TPU v7x, 128 devices: a whole 4x4x4 slice. The times are simulated.
128 devices in a mesh: seg: 8 (over z, core), energy: 16 (over y, x).
Axes of the slice: x: 4, y: 4, z: 4, core: 2. Of those that a mesh axis runs over, the one named last changes fastest.
Arguments:
- green: float32 [16, 32, 2, 256, 256], P('energy', 'seg'), may hold values from -6 to 6
- couple_left: float32 [16, 32, 2, 256, 256], P('energy', 'seg'), may hold values from -0.01171875 to 0.01171875
- couple_right: float32 [16, 32, 2, 256, 256], P('energy', 'seg'), may hold values from -0.01171875 to 0.01171875
- coupling: int32 [16, 32], P('energy', 'seg'), may hold values 0 or 1
- screened: float32 [16, 32, 2, 256, 256], P('energy', 'seg'), may hold values from -1.5 to 1.5
Outputs:
- diagonal: float32 [16, 32, 2, 256, 256], P('energy', 'seg')
- self_energy: float32 [16, 32, 2, 256, 256], P('energy', 'seg')
Inputs may be any that keep to these rules, and one draw needn't show every extreme that they name: `coupling`: 1 where block b is coupled to block b - 1, else 0; the entries of block 0 are not read.
All inputs are finite; a program needn't handle non-finite values.
Results may differ from a plain program's by a relative error of at most 0.0003.
Values sent between devices are 32-bit elements; how exact they have to be, the bound alone decides.
A program may use at most 128 MiB of HBM per device.

v0:
```python
import functools
import math

import jax
import jax.numpy as jnp
from jax import lax
from jax.experimental import pallas as pl
from jax.experimental.pallas import tpu as pltpu
from jax.sharding import PartitionSpec as P

F32 = jnp.float32
BF16 = jnp.bfloat16
MESH = pl.DeviceIdType.MESH

G0, X0, Y0, Z3 = 3, 10, 17, 21
T0, T1, A_IN, C_IN, RS, RP, RQ, U, W, M_IN, CUR = range(25, 36)
PLACES = 36
BLOCKS = 4


def dft(values):
    n = len(values)
    if n == 1:
        return values
    even, odd = dft(values[0::2]), dft(values[1::2])
    out = [None] * n
    half = n // 2
    for j in range(half):
        er, ei = even[j]
        orr, oi = odd[j]
        angle = -2.0 * math.pi * j / n
        cos, sin = math.cos(angle), math.sin(angle)
        if j == 0:
            tr, ti = orr, oi
        elif 4 * j == n:
            tr, ti = oi, -orr
        elif 8 * j == n:
            tr, ti = (orr + oi) * cos, (oi - orr) * cos
        elif 8 * j == 3 * n:
            tr, ti = (oi - orr) * -cos, (orr + oi) * cos
        else:
            tr, ti = orr * cos - oi * sin, orr * sin + oi * cos
        out[j] = (er + tr, ei + ti)
        out[j + half] = (er - tr, ei - ti)
    return out


def kernel(
    ny, nx,
    g_hbm, a_hbm, c_hbm, m_ref, w_hbm, diag_hbm, self_hbm,
    gf, af, cf, zf, sf, pqf, rx, co, mi, oi, dg, rows, srows, res, ops,
    in_sem, sc_sem, x_send, x_recv, ch_sem, fw_sem, a_send, a_recv, r_send, r_recv, out_sem,
):
    ne = ny * nx
    depth = dg.shape[2] // ne
    width = dg.shape[3]
    seg = lax.axis_index("seg")
    me = lax.axis_index("energy")
    z, c = lax.div(seg, 2), lax.rem(seg, 2)
    nz = lax.axis_size("seg") // 2
    last = nz - 1
    my_y, my_x = lax.div(me, nx), lax.rem(me, nx)
    k = c * z + (1 - c) * (last - z)
    partner = seg + 1 - 2 * c
    onward = seg + 4 * c - 2
    high = lax.div(2 * z, nz)

    def peer(offset):
        dy, dx = lax.div(offset, nx), lax.rem(offset, nx)
        return lax.rem(my_y + dy, ny) * nx + lax.rem(my_x + dx, nx)

    def rows_of(energy):
        return pl.ds(pl.multiple_of(energy * depth, depth), depth)

    def load(b):
        return [
            pltpu.make_async_copy(src.at[b], dst.at[b], in_sem.at[b, j])
            for j, (src, dst) in enumerate(((g_hbm, gf), (a_hbm, af), (c_hbm, cf)))
        ]

    for b in range(BLOCKS):
        for copy in load(b):
            copy.start()

    barrier = pltpu.get_barrier_semaphore()

    @pl.loop(1, ne)
    def _(offset):
        pl.semaphore_signal(barrier, inc=1, device_id=(seg, peer(offset)), device_id_type=MESH)

    pl.semaphore_signal(barrier, inc=1, device_id=(partner, me), device_id_type=MESH)

    @pl.when(z > 0)
    def _():
        pl.semaphore_signal(barrier, inc=1, device_id=(seg - 2, me), device_id_type=MESH)

    @pl.when(z < last)
    def _():
        pl.semaphore_signal(barrier, inc=1, device_id=(seg + 2, me), device_id_type=MESH)

    neighbours = lax.div(z + last, nz) + lax.div(last - z + last, nz)
    pl.semaphore_wait(barrier, ne + neighbours)

    @pl.loop(1, ne)
    def _(offset):
        to = peer(offset)
        pltpu.make_async_remote_copy(
            src_ref=w_hbm.at[:, :, rows_of(to), :],
            dst_ref=srows.at[me],
            send_sem=sc_sem.at[0],
            recv_sem=sc_sem.at[1],
            device_id=(seg, to),
            device_id_type=MESH,
        ).start()

    own_screen = pltpu.make_async_copy(w_hbm.at[:, :, rows_of(me), :], srows.at[me], sc_sem.at[2])
    own_screen.start()

    def split_store(place, real, imag):
        for q, value in enumerate((real, imag, real + imag)):
            top = value.astype(BF16)
            ops[place, q, 0] = top
            ops[place, q, 1] = (value - top.astype(F32)).astype(BF16)

    def product(left, right):
        parts = []
        for q in range(3):
            lhs = jnp.concatenate([ops[left, q, 0], ops[left, q, 0], ops[left, q, 1]], axis=1)
            rhs = jnp.concatenate([ops[right, q, 0], ops[right, q, 1], ops[right, q, 0]], axis=0)
            parts.append(jnp.dot(lhs, rhs, preferred_element_type=F32))
        return parts[0] - parts[1], parts[2] - parts[0] - parts[1]

    @pl.loop(0, BLOCKS)
    def _(b):
        for copy in load(b):
            copy.wait()
        weight = m_ref[0, b].astype(F32)
        split_store(G0 - b, gf[b, 0], gf[b, 1])
        split_store(A_IN, af[b, 0] * weight, af[b, 1] * weight)
        split_store(C_IN, cf[b, 0], cf[b, 1])
        split_store(X0 - b, *product(G0 - b, A_IN))
        split_store(Y0 - b, *product(C_IN, G0 - b))
        real, imag = product(C_IN, X0 - b)
        zf[b, 0] = real
        zf[b, 1] = imag

        @pl.when(b == BLOCKS - 1)
        def _():
            split_store(Z3, zf[BLOCKS - 1, 0], zf[BLOCKS - 1, 1])

    @pl.loop(1, BLOCKS)
    def _(i):
        j = BLOCKS - 1 - i
        split_store(T0, *product(X0 - i, G0 + i - 1))
        split_store(T1, *product(Y0 - j, Z3 + i - 1))
        real, imag = product(T0, Y0 - i)
        real, imag = real + gf[i, 0], imag + gf[i, 1]
        sf[0, 0] = real
        sf[0, 1] = imag
        split_store(G0 + i, real, imag)
        real, imag = product(T1, X0 - j)
        real, imag = real + zf[j, 0], imag + zf[j, 1]
        sf[1, 0] = real
        sf[1, 1] = imag
        split_store(Z3 + i, real, imag)

    def exchange(j, src):
        return pltpu.make_async_remote_copy(
            src_ref=src,
            dst_ref=rx.at[j],
            send_sem=x_send.at[j],
            recv_sem=x_recv.at[j],
            device_id=(partner, me),
            device_id_type=MESH,
        )

    swap_source = exchange(0, sf.at[c])
    swap_source.start()

    @pl.loop(1, BLOCKS)
    def _(i):
        real, imag = product(X0 - i, X0 + i - 1)
        pqf[0, 0] = real
        pqf[0, 1] = imag
        split_store(X0 + i, real, imag)
        real, imag = product(Y0 + i - 1, Y0 - i)
        pqf[1, 0] = real
        pqf[1, 1] = imag
        split_store(Y0 + i, real, imag)

    swap_p, swap_q = exchange(1, pqf.at[0]), exchange(2, pqf.at[1])
    swap_p.start()
    swap_q.start()

    own_p, own_q = X0 + BLOCKS - 1, Y0 + BLOCKS - 1
    own_left = c * own_p + (1 - c) * own_q
    own_right = c * own_q + (1 - c) * own_p
    his_left = RP + 1 - c
    his_right = RP + c
    relay = pltpu.make_async_remote_copy(
        src_ref=co, dst_ref=mi, send_sem=ch_sem.at[0], recv_sem=ch_sem.at[1],
        device_id=(onward, me), device_id_type=MESH,
    )
    forward = pltpu.make_async_remote_copy(
        src_ref=mi, dst_ref=oi, send_sem=fw_sem.at[0], recv_sem=fw_sem.at[1],
        device_id=(partner, me), device_id_type=MESH,
    )

    swap_source.wait_recv()
    split_store(RS, rx[0, 0], rx[0, 1])
    split_store(T0, *product(own_left, RS))
    real, imag = product(T0, own_right)
    co[0] = real + sf[1 - c, 0]
    co[1] = imag + sf[1 - c, 1]

    @pl.when(k == 0)
    def _():
        relay.start()

    swap_p.wait_recv()
    swap_q.wait_recv()
    split_store(RP, rx[1, 0], rx[1, 1])
    split_store(RQ, rx[2, 0], rx[2, 1])
    split_store(U, *product(own_left, his_left))
    split_store(W, *product(his_right, own_right))

    def batch(b, sem):
        spot = rows.at[b, pl.ds(0, ne - 1)]
        return pltpu.make_async_copy(spot, spot, sem.at[b])

    def diag_out(b):
        return pltpu.make_async_copy(dg.at[b], diag_hbm.at[b], out_sem.at[0, b])

    def publish(second, b, real, imag):
        @pl.when(second == 0)
        def _():
            dg[b, 0] = real
            dg[b, 1] = imag

        @pl.when(second == 1)
        def _():
            dg[b, 0] = dg[b, 0] + real
            dg[b, 1] = dg[b, 1] + imag

            @pl.loop(1, ne)
            def _(offset):
                to = peer(offset)
                pltpu.make_async_remote_copy(
                    src_ref=dg.at[b, :, rows_of(to), :],
                    dst_ref=rows.at[b, me],
                    send_sem=a_send.at[b],
                    recv_sem=a_recv.at[b],
                    device_id=(seg, to),
                    device_id_type=MESH,
                ).start()

            diag_out(b).start()
            rows[b, me] = dg[b, :, rows_of(me), :]

    tiles = [(r, v) for r in range(0, depth, 8) for v in range(0, width, 128)]

    @pl.loop(0, 2)
    def _(i):
        direction = lax.rem(i + high, 2)
        own = lax.rem(direction + c, 2) == 1

        @pl.when(i == 1)
        def _():
            spot = srows.at[pl.ds(0, ne - 1)]
            pltpu.make_async_copy(spot, spot, sc_sem.at[1]).wait()
            own_screen.wait()

            @pl.loop(0, BLOCKS)
            def _(b):
                for r, v in tiles:
                    at = (pl.ds(r, 8), pl.ds(v, 128))
                    values = dft([(srows[(e, b, 0) + at], srows[(e, b, 1) + at]) for e in range(ne)])
                    for e in range(ne):
                        srows[(e, b, 0) + at] = values[e][0] * (1.0 / ne)
                        srows[(e, b, 1) + at] = values[e][1] * (1.0 / ne)

        @pl.when((i == lax.div(k, last)) & (k > 0))
        def _():
            relay.wait_recv()
            forward.start()
            split_store(M_IN, mi[0], mi[1])

            @pl.when(k < last)
            def _():
                split_store(T0, *product(U, M_IN))
                real, imag = product(T0, W)
                co[0] = co[0] + real
                co[1] = co[1] + imag
                relay.start()

        @pl.when(own & (k > 0))
        def _():
            split_store(T0, *product(his_left, M_IN))
            real, imag = product(T0, his_right)
            split_store(CUR, real + rx[0, 0], imag + rx[0, 1])

        @pl.when(own & (k == 0))
        def _():
            split_store(CUR, rx[0, 0], rx[0, 1])

        @pl.when(jnp.logical_not(own) & (k < last))
        def _():
            forward.wait_recv()
            split_store(CUR, oi[0], oi[1])

        @pl.when(jnp.logical_not(own) & (k == last))
        def _():
            ops[CUR] = jnp.zeros(ops.shape[1:], BF16)

        @pl.when(direction == 0)
        def _():
            @pl.loop(0, BLOCKS)
            def _(b):
                split_store(T0, *product(X0 - b, CUR))
                real, imag = product(T0, Y0 - b)
                real, imag = real + gf[b, 0], imag + gf[b, 1]
                publish(i, b, real, imag)
                split_store(CUR, real, imag)

        @pl.when(direction == 1)
        def _():
            @pl.loop(0, BLOCKS)
            def _(j):
                b = BLOCKS - 1 - j
                split_store(T0, *product(G0 - b, CUR))
                real, imag = product(T0, G0 - b)
                publish(i, b, real, imag)

                @pl.when(b > 0)
                def _():
                    split_store(T1, *product(Y0 - b, CUR))
                    real, imag = product(T1, X0 - b)
                    split_store(CUR, real + zf[b, 0], imag + zf[b, 1])

    def own_self(b):
        return pltpu.make_async_copy(
            res.at[b, me], self_hbm.at[b, :, rows_of(me), :], out_sem.at[1, b]
        )

    @pl.loop(0, BLOCKS)
    def _(j):
        b = high * j + (1 - high) * (BLOCKS - 1 - j)
        batch(b, a_recv).wait()
        for r, v in tiles:
            at = (pl.ds(r, 8), pl.ds(v, 128))
            values = dft([(rows[(b, e, 0) + at], rows[(b, e, 1) + at]) for e in range(ne)])
            mixed = []
            for e in range(ne):
                vr, vi = values[e]
                wr, wi = srows[(e, b, 0) + at], srows[(e, b, 1) + at]
                mixed.append((vr * wi + vi * wr, vr * wr - vi * wi))
            values = dft(mixed)
            for e in range(ne):
                res[(b, e, 0) + at] = values[e][1]
                res[(b, e, 1) + at] = values[e][0]

        @pl.loop(1, ne)
        def _(offset):
            to = peer(offset)
            pltpu.make_async_remote_copy(
                src_ref=res.at[b, to],
                dst_ref=self_hbm.at[b, :, rows_of(me), :],
                send_sem=r_send.at[b],
                recv_sem=r_recv.at[b],
                device_id=(seg, to),
                device_id_type=MESH,
            ).start()

        own_self(b).start()

    @pl.loop(0, BLOCKS)
    def _(b):
        for sem in (a_send, r_send, r_recv):
            batch(b, sem).wait()
        diag_out(b).wait()
        own_self(b).wait()

    spot = srows.at[pl.ds(0, ne - 1)]
    pltpu.make_async_copy(spot, spot, sc_sem.at[0]).wait()
    swap_source.wait_send()
    swap_p.wait_send()
    swap_q.wait_send()

    @pl.when(k < last)
    def _():
        relay.wait_send()

    @pl.when(k > 0)
    def _():
        forward.wait_send()


def per_device(ny, nx, green, couple_left, couple_right, coupling, screened):
    shape = green.shape[1:]
    blocks, _, order, _ = shape
    ne = ny * nx
    depth = order // ne
    one = (2, order, order)
    anywhere = pl.BlockSpec(memory_space=pl.ANY)
    diagonal, self_energy = pl.pallas_call(
        functools.partial(kernel, ny, nx),
        out_shape=[jax.ShapeDtypeStruct(shape, F32)] * 2,
        in_specs=[anywhere] * 3 + [pl.BlockSpec(memory_space=pltpu.SMEM), anywhere],
        out_specs=[anywhere] * 2,
        scratch_shapes=[
            pltpu.VMEM(shape, F32),
            pltpu.VMEM(shape, F32),
            pltpu.VMEM(shape, F32),
            pltpu.VMEM(shape, F32),
            pltpu.VMEM((2,) + one, F32),
            pltpu.VMEM((2,) + one, F32),
            pltpu.VMEM((3,) + one, F32),
            pltpu.VMEM(one, F32),
            pltpu.VMEM(one, F32),
            pltpu.VMEM(one, F32),
            pltpu.VMEM(shape, F32),
            pltpu.VMEM((blocks, ne, 2, depth, order), F32),
            pltpu.VMEM((ne, blocks, 2, depth, order), F32),
            pltpu.VMEM((blocks, ne, 2, depth, order), F32),
            pltpu.VMEM((PLACES, 3, 2, order, order), BF16),
            pltpu.SemaphoreType.DMA((blocks, 3)),
            pltpu.SemaphoreType.DMA((3,)),
            pltpu.SemaphoreType.DMA((3,)),
            pltpu.SemaphoreType.DMA((3,)),
            pltpu.SemaphoreType.DMA((2,)),
            pltpu.SemaphoreType.DMA((2,)),
            pltpu.SemaphoreType.DMA((blocks,)),
            pltpu.SemaphoreType.DMA((blocks,)),
            pltpu.SemaphoreType.DMA((blocks,)),
            pltpu.SemaphoreType.DMA((blocks,)),
            pltpu.SemaphoreType.DMA((2, blocks)),
        ],
        compiler_params=pltpu.CompilerParams(
            collective_id=0, has_side_effects=True, vmem_limit_bytes=60 * 2**20
        ),
    )(green[0], couple_left[0], couple_right[0], coupling, screened[0])
    return diagonal[None], self_energy[None]


def solution(mesh):
    blocks = P("energy", "seg", None, None, None)
    energies = mesh.shape["energy"]
    nx = math.isqrt(energies)
    return jax.shard_map(
        functools.partial(per_device, energies // nx, nx),
        mesh=mesh,
        in_specs=(blocks, blocks, blocks, P("energy", "seg"), blocks),
        out_specs=(blocks, blocks),
        check_vma=False,
    )
```

profile of v0, /device:TPU:1, one launch (start us, length us, event | category | flops | bytes accessed | tf_op | source)
XLA Modules:
  0.0 115.1 jit_solution(161530766001364550)
XLA Ops:
  0.6 109.9 %shard_map.68 = (f32[4,2,256,256]{3,2,1,0:T(8,128)}, f32[4,2,256,256]{3,2,1,0:T(8,128)}) custom-call(f32[4,2,256,256]{3,2,1,0:T(8,128)} %bitcast.8, f32[4,2,256,256]{3,2,1,0:T(8,128)} %bitcast.9, f32[4,2,256,256]{3,2,1,0:T(8,128)} %bitcast.10, s32[1,4]{1,0:T(1,128)} %m_ref.1, f32[4,2,256,256]{3,2,1,0:T(8,128)} %bitcast.11), custom_call_target="tpu_custom_call" | custom-call | tf_op jit(solution)/shard_map/pallas_call | solution.py:405
  110.5 0.0 copy-start
  110.6 3.2 %copy.9 = f32[1,4,2,256,256]{4,3,2,1,0:T(8,128)} copy(f32[1,4,2,256,256]{4,3,2,1,0:T(8,128)} %bitcast.7) | data formatting | bytes 4194304
  113.8 0.0 copy-done
  113.8 1.3 %copy.10 = f32[1,4,2,256,256]{4,3,2,1,0:T(8,128)} copy(f32[1,4,2,256,256]{4,3,2,1,0:T(8,128)S(1)} %bitcast.6) | data formatting | bytes 4194304
Async XLA Ops:
  110.5 3.2 %copy-start = (f32[4,2,256,256]{3,2,1,0:T(8,128)S(1)}, f32[4,2,256,256]{3,2,1,0:T(8,128)}, u32[]{:S(2)}) copy-start(f32[4,2,256,256]{3,2,1,0:T(8,128)} %get-tuple-element.5) | copy-start | bytes 6291460
where the time goes:
time: 115 us
  Pallas kernels  110 us (96%)
  local copies, waits for them, and re-layouts  4.52 us (4%)
    pallas_call x1, Pallas kernels, per_device(): pl.pallas_call(functools.partial(kernel, ny, nx), out_shape=[jax.ShapeDty...  110 us
    unnamed x4, local copies, waits for them, and re-layouts  4.52 us

commit v1 on v0

--- a/solution.py
+++ b/solution.py
@@ -12,9 +12,9 @@
 BF16 = jnp.bfloat16
 MESH = pl.DeviceIdType.MESH
 
-G0, X0, Y0, Z3 = 3, 10, 17, 21
-T0, T1, A_IN, C_IN, RS, RP, RQ, U, W, M_IN, CUR = range(25, 36)
-PLACES = 36
+G0, X0, Y0 = 3, 10, 17
+T0, T1, A_IN, C_IN, RS, RP, RQ, U, W, M_IN, CUR = range(21, 32)
+PLACES = 32
 BLOCKS = 4
 
 
@@ -48,7 +48,7 @@
 def kernel(
     ny, nx,
     g_hbm, a_hbm, c_hbm, m_ref, w_hbm, diag_hbm, self_hbm,
-    gf, af, cf, zf, sf, pqf, rx, co, mi, oi, dg, rows, srows, res, ops,
+    gf, af, cf, sf, pqf, rx, co, mi, oi, dg, rows, srows, res, ops,
     in_sem, sc_sem, x_send, x_recv, ch_sem, fw_sem, a_send, a_recv, r_send, r_recv, out_sem,
 ):
     ne = ny * nx
@@ -135,34 +135,12 @@
         for copy in load(b):
             copy.wait()
         weight = m_ref[0, b].astype(F32)
+        af[b] = af[b] * weight
         split_store(G0 - b, gf[b, 0], gf[b, 1])
-        split_store(A_IN, af[b, 0] * weight, af[b, 1] * weight)
+        split_store(A_IN, af[b, 0], af[b, 1])
         split_store(C_IN, cf[b, 0], cf[b, 1])
         split_store(X0 - b, *product(G0 - b, A_IN))
         split_store(Y0 - b, *product(C_IN, G0 - b))
-        real, imag = product(C_IN, X0 - b)
-        zf[b, 0] = real
-        zf[b, 1] = imag
-
-        @pl.when(b == BLOCKS - 1)
-        def _():
-            split_store(Z3, zf[BLOCKS - 1, 0], zf[BLOCKS - 1, 1])
-
-    @pl.loop(1, BLOCKS)
-    def _(i):
-        j = BLOCKS - 1 - i
-        split_store(T0, *product(X0 - i, G0 + i - 1))
-        split_store(T1, *product(Y0 - j, Z3 + i - 1))
-        real, imag = product(T0, Y0 - i)
-        real, imag = real + gf[i, 0], imag + gf[i, 1]
-        sf[0, 0] = real
-        sf[0, 1] = imag
-        split_store(G0 + i, real, imag)
-        real, imag = product(T1, X0 - j)
-        real, imag = real + zf[j, 0], imag + zf[j, 1]
-        sf[1, 0] = real
-        sf[1, 1] = imag
-        split_store(Z3 + i, real, imag)
 
     def exchange(j, src):
         return pltpu.make_async_remote_copy(
@@ -175,22 +153,7 @@
         )
 
     swap_source = exchange(0, sf.at[c])
-    swap_source.start()
-
-    @pl.loop(1, BLOCKS)
-    def _(i):
-        real, imag = product(X0 - i, X0 + i - 1)
-        pqf[0, 0] = real
-        pqf[0, 1] = imag
-        split_store(X0 + i, real, imag)
-        real, imag = product(Y0 + i - 1, Y0 - i)
-        pqf[1, 0] = real
-        pqf[1, 1] = imag
-        split_store(Y0 + i, real, imag)
-
     swap_p, swap_q = exchange(1, pqf.at[0]), exchange(2, pqf.at[1])
-    swap_p.start()
-    swap_q.start()
 
     own_p, own_q = X0 + BLOCKS - 1, Y0 + BLOCKS - 1
     own_left = c * own_p + (1 - c) * own_q
@@ -206,23 +169,73 @@
         device_id=(partner, me), device_id_type=MESH,
     )
 
-    swap_source.wait_recv()
-    split_store(RS, rx[0, 0], rx[0, 1])
-    split_store(T0, *product(own_left, RS))
-    real, imag = product(T0, own_right)
-    co[0] = real + sf[1 - c, 0]
-    co[1] = imag + sf[1 - c, 1]
-
-    @pl.when(k == 0)
-    def _():
-        relay.start()
-
-    swap_p.wait_recv()
-    swap_q.wait_recv()
-    split_store(RP, rx[1, 0], rx[1, 1])
-    split_store(RQ, rx[2, 0], rx[2, 1])
-    split_store(U, *product(own_left, his_left))
-    split_store(W, *product(his_right, own_right))
+    def chain(direction):
+        @pl.when(direction == 0)
+        def _():
+            @pl.loop(1, BLOCKS)
+            def _(b):
+                split_store(T0, *product(X0 - b, G0 + b - 1))
+                real, imag = product(T0, Y0 - b)
+                real, imag = real + gf[b, 0], imag + gf[b, 1]
+                sf[0, 0] = real
+                sf[0, 1] = imag
+                split_store(G0 + b, real, imag)
+
+        @pl.when(direction == 1)
+        def _():
+            split_store(T1, af[BLOCKS - 1, 0], af[BLOCKS - 1, 1])
+
+            @pl.loop(0, BLOCKS)
+            def _(j):
+                b = BLOCKS - 1 - j
+                real, imag = product(Y0 - b, T1)
+                sf[1, 0] = real
+                sf[1, 1] = imag
+
+                @pl.when(b > 0)
+                def _():
+                    split_store(CUR, real, imag)
+                    real_next, imag_next = product(CUR, X0 - b + 1)
+                    split_store(T1, real_next + af[b - 1, 0], imag_next + af[b - 1, 1])
+
+        @pl.when(direction == c)
+        def _():
+            swap_source.start()
+
+    def outer():
+        @pl.loop(1, BLOCKS)
+        def _(b):
+            real, imag = product(X0 - b, X0 + b - 1)
+            pqf[0, 0] = real
+            pqf[0, 1] = imag
+            split_store(X0 + b, real, imag)
+            real, imag = product(Y0 + b - 1, Y0 - b)
+            pqf[1, 0] = real
+            pqf[1, 1] = imag
+            split_store(Y0 + b, real, imag)
+
+        swap_p.start()
+        swap_q.start()
+
+    def join():
+        swap_source.wait_recv()
+        split_store(RS, rx[0, 0], rx[0, 1])
+        split_store(T0, *product(own_left, RS))
+        real, imag = product(T0, own_right)
+        co[0] = real + sf[1 - c, 0]
+        co[1] = imag + sf[1 - c, 1]
+
+        @pl.when(k == 0)
+        def _():
+            relay.start()
+
+    def compose():
+        swap_p.wait_recv()
+        swap_q.wait_recv()
+        split_store(RP, rx[1, 0], rx[1, 1])
+        split_store(RQ, rx[2, 0], rx[2, 1])
+        split_store(U, *product(own_left, his_left))
+        split_store(W, *product(his_right, own_right))
 
     def batch(b, sem):
         spot = rows.at[b, pl.ds(0, ne - 1)]
@@ -259,39 +272,35 @@
 
     tiles = [(r, v) for r in range(0, depth, 8) for v in range(0, width, 128)]
 
-    @pl.loop(0, 2)
-    def _(i):
-        direction = lax.rem(i + high, 2)
+    def transform_screened():
+        spot = srows.at[pl.ds(0, ne - 1)]
+        pltpu.make_async_copy(spot, spot, sc_sem.at[1]).wait()
+        own_screen.wait()
+
+        @pl.loop(0, BLOCKS)
+        def _(b):
+            for r, v in tiles:
+                at = (pl.ds(r, 8), pl.ds(v, 128))
+                values = dft([(srows[(e, b, 0) + at], srows[(e, b, 1) + at]) for e in range(ne)])
+                for e in range(ne):
+                    srows[(e, b, 0) + at] = values[e][0] * (1.0 / ne)
+                    srows[(e, b, 1) + at] = values[e][1] * (1.0 / ne)
+
+    def pass_on():
+        relay.wait_recv()
+        forward.start()
+        split_store(M_IN, mi[0], mi[1])
+
+        @pl.when(k < last)
+        def _():
+            split_store(T0, *product(U, M_IN))
+            real, imag = product(T0, W)
+            co[0] = co[0] + real
+            co[1] = co[1] + imag
+            relay.start()
+
+    def sweep(second, direction):
         own = lax.rem(direction + c, 2) == 1
-
-        @pl.when(i == 1)
-        def _():
-            spot = srows.at[pl.ds(0, ne - 1)]
-            pltpu.make_async_copy(spot, spot, sc_sem.at[1]).wait()
-            own_screen.wait()
-
-            @pl.loop(0, BLOCKS)
-            def _(b):
-                for r, v in tiles:
-                    at = (pl.ds(r, 8), pl.ds(v, 128))
-                    values = dft([(srows[(e, b, 0) + at], srows[(e, b, 1) + at]) for e in range(ne)])
-                    for e in range(ne):
-                        srows[(e, b, 0) + at] = values[e][0] * (1.0 / ne)
-                        srows[(e, b, 1) + at] = values[e][1] * (1.0 / ne)
-
-        @pl.when((i == lax.div(k, last)) & (k > 0))
-        def _():
-            relay.wait_recv()
-            forward.start()
-            split_store(M_IN, mi[0], mi[1])
-
-            @pl.when(k < last)
-            def _():
-                split_store(T0, *product(U, M_IN))
-                real, imag = product(T0, W)
-                co[0] = co[0] + real
-                co[1] = co[1] + imag
-                relay.start()
 
         @pl.when(own & (k > 0))
         def _():
@@ -319,7 +328,7 @@
                 split_store(T0, *product(X0 - b, CUR))
                 real, imag = product(T0, Y0 - b)
                 real, imag = real + gf[b, 0], imag + gf[b, 1]
-                publish(i, b, real, imag)
+                publish(second, b, real, imag)
                 split_store(CUR, real, imag)
 
         @pl.when(direction == 1)
@@ -329,13 +338,45 @@
                 b = BLOCKS - 1 - j
                 split_store(T0, *product(G0 - b, CUR))
                 real, imag = product(T0, G0 - b)
-                publish(i, b, real, imag)
+                publish(second, b, real, imag)
 
                 @pl.when(b > 0)
                 def _():
-                    split_store(T1, *product(Y0 - b, CUR))
-                    real, imag = product(T1, X0 - b)
-                    split_store(CUR, real + zf[b, 0], imag + zf[b, 1])
+                    real, imag = product(CUR, X0 - b)
+                    split_store(T1, real + af[b, 0], imag + af[b, 1])
+                    split_store(CUR, *product(Y0 - b, T1))
+
+    @pl.loop(0, 4)
+    def _(i):
+        direction = lax.rem(i + high, 2)
+
+        @pl.when(i == 3)
+        def _():
+            transform_screened()
+
+        @pl.when((i == k) & (k > 0))
+        def _():
+            pass_on()
+
+        @pl.when(i < 2)
+        def _():
+            chain(direction)
+
+            @pl.when(i == 0)
+            def _():
+                outer()
+
+            @pl.when(direction != c)
+            def _():
+                join()
+
+            @pl.when(i == 0)
+            def _():
+                compose()
+
+        @pl.when(i >= 2)
+        def _():
+            sweep(i - 2, direction)
 
     def own_self(b):
         return pltpu.make_async_copy(
@@ -408,7 +449,6 @@
         in_specs=[anywhere] * 3 + [pl.BlockSpec(memory_space=pltpu.SMEM), anywhere],
         out_specs=[anywhere] * 2,
         scratch_shapes=[
-            pltpu.VMEM(shape, F32),
             pltpu.VMEM(shape, F32),
             pltpu.VMEM(shape, F32),
             pltpu.VMEM(shape, F32),

time: 115 us -> 110 us (0.957)
  Pallas kernels: 110 us -> 105 us
    pallas_call x1, Pallas kernels: 110 us -> 105 us  [per_device(): pl.pallas_call(functools.partial(kernel, ny, nx), out_shape=[jax.ShapeDty...]
where the time goes in v1:
time: 110 us
  Pallas kernels  105 us (95%)
  local copies, waits for them, and re-layouts  4.52 us (4%)
    pallas_call x1, Pallas kernels, per_device(): pl.pallas_call(functools.partial(kernel, ny, nx), out_shape=[jax.ShapeDty...  105 us
    unnamed x4, local copies, waits for them, and re-layouts  4.52 us

profile of v1, /device:TPU:1, one launch (start us, length us, event | category | flops | bytes accessed | tf_op | source)
XLA Modules:
  0.0 110.1 jit_solution(8238125135447089741)
XLA Ops:
  0.6 104.9 %shard_map.68 = (f32[4,2,256,256]{3,2,1,0:T(8,128)}, f32[4,2,256,256]{3,2,1,0:T(8,128)}) custom-call(f32[4,2,256,256]{3,2,1,0:T(8,128)} %bitcast.8, f32[4,2,256,256]{3,2,1,0:T(8,128)} %bitcast.9, f32[4,2,256,256]{3,2,1,0:T(8,128)} %bitcast.10, s32[1,4]{1,0:T(1,128)} %m_ref.1, f32[4,2,256,256]{3,2,1,0:T(8,128)} %bitcast.11), custom_call_target="tpu_custom_call" | custom-call | tf_op jit(solution)/shard_map/pallas_call | solution.py:446
  105.6 0.0 copy-start
  105.6 3.2 %copy.9 = f32[1,4,2,256,256]{4,3,2,1,0:T(8,128)} copy(f32[1,4,2,256,256]{4,3,2,1,0:T(8,128)} %bitcast.7) | data formatting | bytes 4194304
  108.8 0.0 copy-done
  108.8 1.3 %copy.10 = f32[1,4,2,256,256]{4,3,2,1,0:T(8,128)} copy(f32[1,4,2,256,256]{4,3,2,1,0:T(8,128)S(1)} %bitcast.6) | data formatting | bytes 4194304
Async XLA Ops:
  105.6 3.2 %copy-start = (f32[4,2,256,256]{3,2,1,0:T(8,128)S(1)}, f32[4,2,256,256]{3,2,1,0:T(8,128)}, u32[]{:S(2)}) copy-start(f32[4,2,256,256]{3,2,1,0:T(8,128)} %get-tuple-element.5) | copy-start | bytes 6291460

commit v2 on v1

--- a/solution.py
+++ b/solution.py
@@ -130,8 +130,8 @@
             parts.append(jnp.dot(lhs, rhs, preferred_element_type=F32))
         return parts[0] - parts[1], parts[2] - parts[0] - parts[1]
 
-    @pl.loop(0, BLOCKS)
-    def _(b):
+    dg[...] = jnp.zeros(dg.shape, F32)
+    for b in range(BLOCKS):
         for copy in load(b):
             copy.wait()
         weight = m_ref[0, b].astype(F32)
@@ -169,53 +169,48 @@
         device_id=(partner, me), device_id_type=MESH,
     )
 
-    def chain(direction):
-        @pl.when(direction == 0)
-        def _():
-            @pl.loop(1, BLOCKS)
-            def _(b):
+    def chain(direction, outer):
+        for b in range(BLOCKS):
+            j = BLOCKS - 1 - b
+            if direction == 0 and b > 0:
                 split_store(T0, *product(X0 - b, G0 + b - 1))
+            if direction == 1 and b == 0:
+                split_store(T1, af[j, 0], af[j, 1])
+            if direction == 1 and b > 0:
+                real, imag = product(CUR, X0 - j)
+                split_store(T1, real + af[j, 0], imag + af[j, 1])
+            if outer and b > 0:
+                real, imag = product(X0 - b, X0 + b - 1)
+                split_store(X0 + b, real, imag)
+                if b == BLOCKS - 1:
+                    pqf[0, 0] = real
+                    pqf[0, 1] = imag
+            if direction == 0 and b > 0:
                 real, imag = product(T0, Y0 - b)
                 real, imag = real + gf[b, 0], imag + gf[b, 1]
-                sf[0, 0] = real
-                sf[0, 1] = imag
-                split_store(G0 + b, real, imag)
-
-        @pl.when(direction == 1)
-        def _():
-            split_store(T1, af[BLOCKS - 1, 0], af[BLOCKS - 1, 1])
-
-            @pl.loop(0, BLOCKS)
-            def _(j):
-                b = BLOCKS - 1 - j
-                real, imag = product(Y0 - b, T1)
-                sf[1, 0] = real
-                sf[1, 1] = imag
-
-                @pl.when(b > 0)
-                def _():
+                if b < BLOCKS - 1:
+                    split_store(G0 + b, real, imag)
+            if direction == 1:
+                real, imag = product(Y0 - j, T1)
+                if b < BLOCKS - 1:
                     split_store(CUR, real, imag)
-                    real_next, imag_next = product(CUR, X0 - b + 1)
-                    split_store(T1, real_next + af[b - 1, 0], imag_next + af[b - 1, 1])
-
-        @pl.when(direction == c)
+            if b == BLOCKS - 1:
+                sf[direction, 0] = real
+                sf[direction, 1] = imag
+            if outer and b > 0:
+                real, imag = product(Y0 + b - 1, Y0 - b)
+                split_store(Y0 + b, real, imag)
+                if b == BLOCKS - 1:
+                    pqf[1, 0] = real
+                    pqf[1, 1] = imag
+
+        if outer:
+            swap_p.start()
+            swap_q.start()
+
+        @pl.when(c == direction)
         def _():
             swap_source.start()
-
-    def outer():
-        @pl.loop(1, BLOCKS)
-        def _(b):
-            real, imag = product(X0 - b, X0 + b - 1)
-            pqf[0, 0] = real
-            pqf[0, 1] = imag
-            split_store(X0 + b, real, imag)
-            real, imag = product(Y0 + b - 1, Y0 - b)
-            pqf[1, 0] = real
-            pqf[1, 1] = imag
-            split_store(Y0 + b, real, imag)
-
-        swap_p.start()
-        swap_q.start()
 
     def join():
         swap_source.wait_recv()
@@ -245,16 +240,11 @@
         return pltpu.make_async_copy(dg.at[b], diag_hbm.at[b], out_sem.at[0, b])
 
     def publish(second, b, real, imag):
-        @pl.when(second == 0)
-        def _():
-            dg[b, 0] = real
-            dg[b, 1] = imag
+        dg[b, 0] = dg[b, 0] + real
+        dg[b, 1] = dg[b, 1] + imag
 
         @pl.when(second == 1)
         def _():
-            dg[b, 0] = dg[b, 0] + real
-            dg[b, 1] = dg[b, 1] + imag
-
             @pl.loop(1, ne)
             def _(offset):
                 to = peer(offset)
@@ -323,60 +313,54 @@
 
         @pl.when(direction == 0)
         def _():
-            @pl.loop(0, BLOCKS)
-            def _(b):
+            for b in range(BLOCKS):
                 split_store(T0, *product(X0 - b, CUR))
                 real, imag = product(T0, Y0 - b)
                 real, imag = real + gf[b, 0], imag + gf[b, 1]
+                if b < BLOCKS - 1:
+                    split_store(CUR, real, imag)
                 publish(second, b, real, imag)
-                split_store(CUR, real, imag)
 
         @pl.when(direction == 1)
         def _():
-            @pl.loop(0, BLOCKS)
-            def _(j):
-                b = BLOCKS - 1 - j
+            for b in reversed(range(BLOCKS)):
                 split_store(T0, *product(G0 - b, CUR))
-                real, imag = product(T0, G0 - b)
-                publish(second, b, real, imag)
-
-                @pl.when(b > 0)
-                def _():
+                if b > 0:
                     real, imag = product(CUR, X0 - b)
                     split_store(T1, real + af[b, 0], imag + af[b, 1])
+                publish(second, b, *product(T0, G0 - b))
+                if b > 0:
                     split_store(CUR, *product(Y0 - b, T1))
 
-    @pl.loop(0, 4)
+    for i in range(2):
+        if i == 1:
+            @pl.when(k == 1)
+            def _():
+                pass_on()
+
+        for side in range(2):
+            @pl.when(high == side)
+            def _():
+                chain((i + side) % 2, i == 0)
+
+        @pl.when(lax.rem(i + high + c, 2) == 1)
+        def _():
+            join()
+
+        if i == 0:
+            compose()
+
+    @pl.loop(2, 4)
     def _(i):
-        direction = lax.rem(i + high, 2)
-
         @pl.when(i == 3)
         def _():
             transform_screened()
 
-        @pl.when((i == k) & (k > 0))
+        @pl.when(i == k)
         def _():
             pass_on()
 
-        @pl.when(i < 2)
-        def _():
-            chain(direction)
-
-            @pl.when(i == 0)
-            def _():
-                outer()
-
-            @pl.when(direction != c)
-            def _():
-                join()
-
-            @pl.when(i == 0)
-            def _():
-                compose()
-
-        @pl.when(i >= 2)
-        def _():
-            sweep(i - 2, direction)
+        sweep(i - 2, lax.rem(i + high, 2))
 
     def own_self(b):
         return pltpu.make_async_copy(

time: 110 us -> 106 us (0.964)
  Pallas kernels: 105 us -> 101 us
    pallas_call x1, Pallas kernels: 105 us -> 101 us  [per_device(): pl.pallas_call(functools.partial(kernel, ny, nx), out_shape=[jax.ShapeDty...]
where the time goes in v2:
time: 106 us
  Pallas kernels  101 us (95%)
  local copies, waits for them, and re-layouts  4.52 us (4%)
    pallas_call x1, Pallas kernels, per_device(): pl.pallas_call(functools.partial(kernel, ny, nx), out_shape=[jax.ShapeDty...  101 us
    unnamed x4, local copies, waits for them, and re-layouts  4.52 us

profile of v2, /device:TPU:1, one launch (start us, length us, event | category | flops | bytes accessed | tf_op | source)
XLA Modules:
  0.0 106.0 jit_solution(3398279634334435373)
XLA Ops:
  0.6 100.9 %shard_map.68 = (f32[4,2,256,256]{3,2,1,0:T(8,128)}, f32[4,2,256,256]{3,2,1,0:T(8,128)}) custom-call(f32[4,2,256,256]{3,2,1,0:T(8,128)} %bitcast.8, f32[4,2,256,256]{3,2,1,0:T(8,128)} %bitcast.9, f32[4,2,256,256]{3,2,1,0:T(8,128)} %bitcast.10, s32[1,4]{1,0:T(1,128)} %m_ref.1, f32[4,2,256,256]{3,2,1,0:T(8,128)} %bitcast.11), custom_call_target="tpu_custom_call" | custom-call | tf_op jit(solution)/shard_map/pallas_call | solution.py:430
  101.5 0.0 copy-start
  101.5 3.2 %copy.9 = f32[1,4,2,256,256]{4,3,2,1,0:T(8,128)} copy(f32[1,4,2,256,256]{4,3,2,1,0:T(8,128)} %bitcast.7) | data formatting | bytes 4194304
  104.7 0.0 copy-done
  104.7 1.3 %copy.10 = f32[1,4,2,256,256]{4,3,2,1,0:T(8,128)} copy(f32[1,4,2,256,256]{4,3,2,1,0:T(8,128)S(1)} %bitcast.6) | data formatting | bytes 4194304
Async XLA Ops:
  101.5 3.2 %copy-start = (f32[4,2,256,256]{3,2,1,0:T(8,128)S(1)}, f32[4,2,256,256]{3,2,1,0:T(8,128)}, u32[]{:S(2)}) copy-start(f32[4,2,256,256]{3,2,1,0:T(8,128)} %get-tuple-element.5) | copy-start | bytes 6291460

commit v3 on v2

--- a/solution.py
+++ b/solution.py
@@ -98,6 +98,32 @@
     def _():
         pl.semaphore_signal(barrier, inc=1, device_id=(seg + 2, me), device_id_type=MESH)
 
+    def split_store(place, real, imag):
+        for q, value in enumerate((real, imag, real + imag)):
+            top = value.astype(BF16)
+            ops[place, q, 0] = top
+            ops[place, q, 1] = (value - top.astype(F32)).astype(BF16)
+
+    def product(left, right):
+        parts = []
+        for q in range(3):
+            lhs = jnp.concatenate([ops[left, q, 0], ops[left, q, 0], ops[left, q, 1]], axis=1)
+            rhs = jnp.concatenate([ops[right, q, 0], ops[right, q, 1], ops[right, q, 0]], axis=0)
+            parts.append(jnp.dot(lhs, rhs, preferred_element_type=F32))
+        return parts[0] - parts[1], parts[2] - parts[0] - parts[1]
+
+    dg[...] = jnp.zeros(dg.shape, F32)
+    for b in range(BLOCKS):
+        for copy in load(b):
+            copy.wait()
+        weight = m_ref[0, b].astype(F32)
+        af[b] = af[b] * weight
+        split_store(G0 - b, gf[b, 0], gf[b, 1])
+        split_store(A_IN, af[b, 0], af[b, 1])
+        split_store(C_IN, cf[b, 0], cf[b, 1])
+        split_store(X0 - b, *product(G0 - b, A_IN))
+        split_store(Y0 - b, *product(C_IN, G0 - b))
+
     neighbours = lax.div(z + last, nz) + lax.div(last - z + last, nz)
     pl.semaphore_wait(barrier, ne + neighbours)
 
@@ -115,32 +141,6 @@
 
     own_screen = pltpu.make_async_copy(w_hbm.at[:, :, rows_of(me), :], srows.at[me], sc_sem.at[2])
     own_screen.start()
-
-    def split_store(place, real, imag):
-        for q, value in enumerate((real, imag, real + imag)):
-            top = value.astype(BF16)
-            ops[place, q, 0] = top
-            ops[place, q, 1] = (value - top.astype(F32)).astype(BF16)
-
-    def product(left, right):
-        parts = []
-        for q in range(3):
-            lhs = jnp.concatenate([ops[left, q, 0], ops[left, q, 0], ops[left, q, 1]], axis=1)
-            rhs = jnp.concatenate([ops[right, q, 0], ops[right, q, 1], ops[right, q, 0]], axis=0)
-            parts.append(jnp.dot(lhs, rhs, preferred_element_type=F32))
-        return parts[0] - parts[1], parts[2] - parts[0] - parts[1]
-
-    dg[...] = jnp.zeros(dg.shape, F32)
-    for b in range(BLOCKS):
-        for copy in load(b):
-            copy.wait()
-        weight = m_ref[0, b].astype(F32)
-        af[b] = af[b] * weight
-        split_store(G0 - b, gf[b, 0], gf[b, 1])
-        split_store(A_IN, af[b, 0], af[b, 1])
-        split_store(C_IN, cf[b, 0], cf[b, 1])
-        split_store(X0 - b, *product(G0 - b, A_IN))
-        split_store(Y0 - b, *product(C_IN, G0 - b))
 
     def exchange(j, src):
         return pltpu.make_async_remote_copy(
@@ -352,15 +352,13 @@
 
     @pl.loop(2, 4)
     def _(i):
-        @pl.when(i == 3)
-        def _():
-            transform_screened()
-
         @pl.when(i == k)
         def _():
             pass_on()
 
         sweep(i - 2, lax.rem(i + high, 2))
+
+    transform_screened()
 
     def own_self(b):
         return pltpu.make_async_copy(
@@ -418,6 +416,18 @@
     @pl.when(k > 0)
     def _():
         forward.wait_send()
+
+
+def hand_over(diag_in, self_in, diag_hbm, self_hbm, sem):
+    copies = [
+        pltpu.make_async_copy(src.at[b], dst.at[b], sem.at[j, b])
+        for b in range(BLOCKS)
+        for j, (src, dst) in enumerate(((diag_in, diag_hbm), (self_in, self_hbm)))
+    ]
+    for copy in copies:
+        copy.start()
+    for copy in copies:
+        copy.wait()
 
 
 def per_device(ny, nx, green, couple_left, couple_right, coupling, screened):
@@ -460,9 +470,17 @@
             pltpu.SemaphoreType.DMA((2, blocks)),
         ],
         compiler_params=pltpu.CompilerParams(
-            collective_id=0, has_side_effects=True, vmem_limit_bytes=60 * 2**20
+            collective_id=0, has_side_effects=True, vmem_limit_bytes=48 * 2**20
         ),
     )(green[0], couple_left[0], couple_right[0], coupling, screened[0])
+    diagonal, self_energy = pl.pallas_call(
+        hand_over,
+        out_shape=[jax.ShapeDtypeStruct(shape, F32)] * 2,
+        in_specs=[anywhere] * 2,
+        out_specs=[anywhere] * 2,
+        scratch_shapes=[pltpu.SemaphoreType.DMA((2, blocks))],
+        compiler_params=pltpu.CompilerParams(vmem_limit_bytes=2**21),
+    )(diagonal, self_energy)
     return diagonal[None], self_energy[None]
 
 

time: 106 us -> 102 us (0.962)
  local copies, waits for them, and re-layouts: 4.52 us -> 0.65 us
    unnamed x4 -> x2, local copies, waits for them, and re-layouts: 4.52 us -> 0.65 us
    pallas_call x1, Pallas kernels: 101 us -> 98.3 us  [per_device(): pl.pallas_call(functools.partial(kernel, ny, nx), out_shape=[jax.ShapeDty...]
    pallas_call x0 -> x1, Pallas kernels: none -> 2.07 us  [per_device(): pl.pallas_call(hand_over, out_shape=[jax.ShapeDtypeStruct(shape, F32)] *...]
where the time goes in v3:
time: 102 us
  Pallas kernels  100 us (98%)
    pallas_call x1, Pallas kernels, per_device(): pl.pallas_call(functools.partial(kernel, ny, nx), out_shape=[jax.ShapeDty...  98.3 us
    pallas_call x1, Pallas kernels, per_device(): pl.pallas_call(hand_over, out_shape=[jax.ShapeDtypeStruct(shape, F32)] *...  2.07 us

profile of v3, /device:TPU:1, one launch (start us, length us, event | category | flops | bytes accessed | tf_op | source)
XLA Modules:
  0.0 101.8 jit_solution(14597631758305494800)
XLA Ops:
  0.6 0.0 copy-start
  0.6 0.6 copy-done
  1.3 98.3 %shard_map.68 = (f32[4,2,256,256]{3,2,1,0:T(8,128)S(1)}, f32[4,2,256,256]{3,2,1,0:T(8,128)S(1)}) custom-call(f32[4,2,256,256]{3,2,1,0:T(8,128)} %bitcast.6, f32[4,2,256,256]{3,2,1,0:T(8,128)} %bitcast.7, f32[4,2,256,256]{3,2,1,0:T(8,128)} %bitcast.8, s32[1,4]{1,0:T(1,128)S(1)} %copy-done, f32[4,2,256,256]{3,2,1,0:T(8,128)} %bitcast.9), custom_call_target="tpu_custom_call" | custom-call | tf_op jit(solution)/shard_map/pallas_call | solution.py:440
  99.6 2.1 %shard_map.69 = (f32[4,2,256,256]{3,2,1,0:T(8,128)}, f32[4,2,256,256]{3,2,1,0:T(8,128)}) custom-call(f32[4,2,256,256]{3,2,1,0:T(8,128)S(1)} %get-tuple-element.6.diag_in, f32[4,2,256,256]{3,2,1,0:T(8,128)S(1)} %get-tuple-element.7.self_in), custom_call_target="tpu_custom_call" | custom-call | tf_op jit(solution)/shard_map/pallas_call | solution.py:476
Async XLA Ops:
  0.6 0.7 copy-start

commit v4 on v3

--- a/solution.py
+++ b/solution.py
@@ -98,18 +98,24 @@
     def _():
         pl.semaphore_signal(barrier, inc=1, device_id=(seg + 2, me), device_id_type=MESH)
 
-    def split_store(place, real, imag):
+    def split_store(place, real, imag, rows_in=slice(None)):
         for q, value in enumerate((real, imag, real + imag)):
             top = value.astype(BF16)
-            ops[place, q, 0] = top
-            ops[place, q, 1] = (value - top.astype(F32)).astype(BF16)
-
-    def product(left, right):
+            ops[place, q, 0, rows_in] = top
+            ops[place, q, 1, rows_in] = (value - top.astype(F32)).astype(BF16)
+
+    def product(left, right, rows_in=slice(None), inner=slice(None)):
         parts = []
         for q in range(3):
-            lhs = jnp.concatenate([ops[left, q, 0], ops[left, q, 0], ops[left, q, 1]], axis=1)
-            rhs = jnp.concatenate([ops[right, q, 0], ops[right, q, 1], ops[right, q, 0]], axis=0)
-            parts.append(jnp.dot(lhs, rhs, preferred_element_type=F32))
+            lhs = [ops[left, q, part, rows_in, inner] for part in (0, 0, 1)]
+            rhs = [ops[right, q, part, inner] for part in (0, 1, 0)]
+            parts.append(
+                jnp.dot(
+                    jnp.concatenate(lhs, axis=1),
+                    jnp.concatenate(rhs, axis=0),
+                    preferred_element_type=F32,
+                )
+            )
         return parts[0] - parts[1], parts[2] - parts[0] - parts[1]
 
     dg[...] = jnp.zeros(dg.shape, F32)
@@ -160,14 +166,24 @@
     own_right = c * own_q + (1 - c) * own_p
     his_left = RP + 1 - c
     his_right = RP + c
-    relay = pltpu.make_async_remote_copy(
-        src_ref=co, dst_ref=mi, send_sem=ch_sem.at[0], recv_sem=ch_sem.at[1],
-        device_id=(onward, me), device_id_type=MESH,
-    )
-    forward = pltpu.make_async_remote_copy(
-        src_ref=mi, dst_ref=oi, send_sem=fw_sem.at[0], recv_sem=fw_sem.at[1],
-        device_id=(partner, me), device_id_type=MESH,
-    )
+    order = dg.shape[2]
+    halves = [slice(h * order // 2, (h + 1) * order // 2) for h in range(2)]
+    relay = [
+        pltpu.make_async_remote_copy(
+            src_ref=co.at[:, half], dst_ref=mi.at[:, half],
+            send_sem=ch_sem.at[0, h], recv_sem=ch_sem.at[1, h],
+            device_id=(onward, me), device_id_type=MESH,
+        )
+        for h, half in enumerate(halves)
+    ]
+    forward = [
+        pltpu.make_async_remote_copy(
+            src_ref=mi.at[:, half], dst_ref=oi.at[:, half],
+            send_sem=fw_sem.at[0, h], recv_sem=fw_sem.at[1, h],
+            device_id=(partner, me), device_id_type=MESH,
+        )
+        for h, half in enumerate(halves)
+    ]
 
     def chain(direction, outer):
         for b in range(BLOCKS):
@@ -216,21 +232,30 @@
         swap_source.wait_recv()
         split_store(RS, rx[0, 0], rx[0, 1])
         split_store(T0, *product(own_left, RS))
-        real, imag = product(T0, own_right)
-        co[0] = real + sf[1 - c, 0]
-        co[1] = imag + sf[1 - c, 1]
-
-        @pl.when(k == 0)
-        def _():
-            relay.start()
+        for h, half in enumerate(halves):
+            real, imag = product(T0, own_right, half)
+            co[0, half] = real + sf[1 - c, 0, half]
+            co[1, half] = imag + sf[1 - c, 1, half]
+
+            @pl.when(k == 0)
+            def _():
+                relay[h].start()
 
     def compose():
         swap_p.wait_recv()
         swap_q.wait_recv()
         split_store(RP, rx[1, 0], rx[1, 1])
         split_store(RQ, rx[2, 0], rx[2, 1])
-        split_store(U, *product(own_left, his_left))
-        split_store(W, *product(his_right, own_right))
+
+        @pl.when(k < last)
+        def _():
+            split_store(U, *product(own_left, his_left))
+            split_store(W, *product(his_right, own_right))
+
+        @pl.when(k == last)
+        def _():
+            ops[U] = ops[his_left]
+            ops[W] = ops[his_right]
 
     def batch(b, sem):
         spot = rows.at[b, pl.ds(0, ne - 1)]
@@ -277,22 +302,32 @@
                     srows[(e, b, 1) + at] = values[e][1] * (1.0 / ne)
 
     def pass_on():
-        relay.wait_recv()
-        forward.start()
-        split_store(M_IN, mi[0], mi[1])
-
-        @pl.when(k < last)
-        def _():
-            split_store(T0, *product(U, M_IN))
-            real, imag = product(T0, W)
-            co[0] = co[0] + real
-            co[1] = co[1] + imag
-            relay.start()
+        @pl.when(k == last)
+        def _():
+            co[...] = rx[0]
+
+        for h, half in enumerate(halves):
+            relay[h].wait_recv()
+            forward[h].start()
+            split_store(M_IN, mi[0, half], mi[1, half], half)
+            split_store(T0, *product(M_IN, W, half), half)
+            for g, other in enumerate(halves):
+                real, imag = product(U, T0, other, half)
+                co[0, other] = co[0, other] + real
+                co[1, other] = co[1, other] + imag
+                if h == 1:
+                    @pl.when(k < last)
+                    def _():
+                        relay[g].start()
 
     def sweep(second, direction):
         own = lax.rem(direction + c, 2) == 1
 
-        @pl.when(own & (k > 0))
+        @pl.when(own & (k == last))
+        def _():
+            split_store(CUR, co[0], co[1])
+
+        @pl.when(own & (k > 0) & (k < last))
         def _():
             split_store(T0, *product(his_left, M_IN))
             real, imag = product(T0, his_right)
@@ -304,7 +339,8 @@
 
         @pl.when(jnp.logical_not(own) & (k < last))
         def _():
-            forward.wait_recv()
+            for half in forward:
+                half.wait_recv()
             split_store(CUR, oi[0], oi[1])
 
         @pl.when(jnp.logical_not(own) & (k == last))
@@ -333,15 +369,15 @@
                     split_store(CUR, *product(Y0 - b, T1))
 
     for i in range(2):
+        for side in range(2):
+            @pl.when(high == side)
+            def _():
+                chain((i + side) % 2, i == 0)
+
         if i == 1:
             @pl.when(k == 1)
             def _():
                 pass_on()
-
-        for side in range(2):
-            @pl.when(high == side)
-            def _():
-                chain((i + side) % 2, i == 0)
 
         @pl.when(lax.rem(i + high + c, 2) == 1)
         def _():
@@ -411,11 +447,13 @@
 
     @pl.when(k < last)
     def _():
-        relay.wait_send()
+        for half in relay:
+            half.wait_send()
 
     @pl.when(k > 0)
     def _():
-        forward.wait_send()
+        for half in forward:
+            half.wait_send()
 
 
 def hand_over(diag_in, self_in, diag_hbm, self_hbm, sem):
@@ -461,8 +499,8 @@
             pltpu.SemaphoreType.DMA((3,)),
             pltpu.SemaphoreType.DMA((3,)),
             pltpu.SemaphoreType.DMA((3,)),
-            pltpu.SemaphoreType.DMA((2,)),
-            pltpu.SemaphoreType.DMA((2,)),
+            pltpu.SemaphoreType.DMA((2, 2)),
+            pltpu.SemaphoreType.DMA((2, 2)),
             pltpu.SemaphoreType.DMA((blocks,)),
             pltpu.SemaphoreType.DMA((blocks,)),
             pltpu.SemaphoreType.DMA((blocks,)),

time: 102 us -> 101 us (level)
    pallas_call x1, Pallas kernels: 98.3 us -> 97 us  [per_device(): pl.pallas_call(functools.partial(kernel, ny, nx), out_shape=[jax.ShapeDty...]
where the time goes in v4:
time: 101 us
  Pallas kernels  99.1 us (98%)
    pallas_call x1, Pallas kernels, per_device(): pl.pallas_call(functools.partial(kernel, ny, nx), out_shape=[jax.ShapeDty...  97 us
    pallas_call x1, Pallas kernels, per_device(): pl.pallas_call(hand_over, out_shape=[jax.ShapeDtypeStruct(shape, F32)] *...  2.07 us

profile of v4, /device:TPU:1, one launch (start us, length us, event | category | flops | bytes accessed | tf_op | source)
XLA Modules:
  0.0 100.6 jit_solution(14092640128390331659)
XLA Ops:
  0.6 0.0 copy-start
  0.6 0.6 copy-done
  1.3 97.0 %shard_map.68 = (f32[4,2,256,256]{3,2,1,0:T(8,128)S(1)}, f32[4,2,256,256]{3,2,1,0:T(8,128)S(1)}) custom-call(f32[4,2,256,256]{3,2,1,0:T(8,128)} %bitcast.6, f32[4,2,256,256]{3,2,1,0:T(8,128)} %bitcast.7, f32[4,2,256,256]{3,2,1,0:T(8,128)} %bitcast.8, s32[1,4]{1,0:T(1,128)S(1)} %copy-done, f32[4,2,256,256]{3,2,1,0:T(8,128)} %bitcast.9), custom_call_target="tpu_custom_call" | custom-call | tf_op jit(solution)/shard_map/pallas_call | solution.py:478
  98.3 2.1 %shard_map.69 = (f32[4,2,256,256]{3,2,1,0:T(8,128)}, f32[4,2,256,256]{3,2,1,0:T(8,128)}) custom-call(f32[4,2,256,256]{3,2,1,0:T(8,128)S(1)} %get-tuple-element.6.diag_in, f32[4,2,256,256]{3,2,1,0:T(8,128)S(1)} %get-tuple-element.7.self_in), custom_call_target="tpu_custom_call" | custom-call | tf_op jit(solution)/shard_map/pallas_call | solution.py:514
Async XLA Ops:
  0.6 0.7 copy-start

commit v5 on v4

--- a/solution.py
+++ b/solution.py
@@ -65,8 +65,11 @@
     onward = seg + 4 * c - 2
     high = lax.div(2 * z, nz)
 
-    def peer(offset):
-        dy, dx = lax.div(offset, nx), lax.rem(offset, nx)
+    def stride(j, n):
+        return lax.rem(2 - j + 3 * lax.div(j, 2) - 2 * lax.div(j, 3), 4) if n == 4 else n - 1 - j
+
+    def peer(turn):
+        dy, dx = stride(lax.div(turn, nx), ny), stride(lax.rem(turn, nx), nx)
         return lax.rem(my_y + dy, ny) * nx + lax.rem(my_x + dx, nx)
 
     def rows_of(energy):
@@ -83,10 +86,6 @@
             copy.start()
 
     barrier = pltpu.get_barrier_semaphore()
-
-    @pl.loop(1, ne)
-    def _(offset):
-        pl.semaphore_signal(barrier, inc=1, device_id=(seg, peer(offset)), device_id_type=MESH)
 
     pl.semaphore_signal(barrier, inc=1, device_id=(partner, me), device_id_type=MESH)
 
@@ -127,26 +126,28 @@
         split_store(G0 - b, gf[b, 0], gf[b, 1])
         split_store(A_IN, af[b, 0], af[b, 1])
         split_store(C_IN, cf[b, 0], cf[b, 1])
+        for energy in range(b * (ne - 1) // BLOCKS, (b + 1) * (ne - 1) // BLOCKS):
+            other = lax.rem(me + 1 + energy, ne)
+            pl.semaphore_signal(barrier, inc=1, device_id=(seg, other), device_id_type=MESH)
         split_store(X0 - b, *product(G0 - b, A_IN))
         split_store(Y0 - b, *product(C_IN, G0 - b))
 
     neighbours = lax.div(z + last, nz) + lax.div(last - z + last, nz)
-    pl.semaphore_wait(barrier, ne + neighbours)
-
-    @pl.loop(1, ne)
-    def _(offset):
-        to = peer(offset)
-        pltpu.make_async_remote_copy(
-            src_ref=w_hbm.at[:, :, rows_of(to), :],
-            dst_ref=srows.at[me],
-            send_sem=sc_sem.at[0],
-            recv_sem=sc_sem.at[1],
-            device_id=(seg, to),
-            device_id_type=MESH,
-        ).start()
-
     own_screen = pltpu.make_async_copy(w_hbm.at[:, :, rows_of(me), :], srows.at[me], sc_sem.at[2])
     own_screen.start()
+
+    def send_screened():
+        @pl.loop(0, ne - 1)
+        def _(turn):
+            to = peer(turn)
+            pltpu.make_async_remote_copy(
+                src_ref=w_hbm.at[:, :, rows_of(to), :],
+                dst_ref=srows.at[me],
+                send_sem=sc_sem.at[0],
+                recv_sem=sc_sem.at[1],
+                device_id=(seg, to),
+                device_id_type=MESH,
+            ).start()
 
     def exchange(j, src):
         return pltpu.make_async_remote_copy(
@@ -220,14 +221,6 @@
                     pqf[1, 0] = real
                     pqf[1, 1] = imag
 
-        if outer:
-            swap_p.start()
-            swap_q.start()
-
-        @pl.when(c == direction)
-        def _():
-            swap_source.start()
-
     def join():
         swap_source.wait_recv()
         split_store(RS, rx[0, 0], rx[0, 1])
@@ -270,9 +263,9 @@
 
         @pl.when(second == 1)
         def _():
-            @pl.loop(1, ne)
-            def _(offset):
-                to = peer(offset)
+            @pl.loop(0, ne - 1)
+            def _(turn):
+                to = peer(turn)
                 pltpu.make_async_remote_copy(
                     src_ref=dg.at[b, :, rows_of(to), :],
                     dst_ref=rows.at[b, me],
@@ -361,11 +354,10 @@
         def _():
             for b in reversed(range(BLOCKS)):
                 split_store(T0, *product(G0 - b, CUR))
+                publish(second, b, *product(T0, G0 - b))
                 if b > 0:
                     real, imag = product(CUR, X0 - b)
                     split_store(T1, real + af[b, 0], imag + af[b, 1])
-                publish(second, b, *product(T0, G0 - b))
-                if b > 0:
                     split_store(CUR, *product(Y0 - b, T1))
 
     for i in range(2):
@@ -374,6 +366,17 @@
             def _():
                 chain((i + side) % 2, i == 0)
 
+        if i == 0:
+            pl.semaphore_wait(barrier, ne + neighbours)
+
+        @pl.when(lax.rem(i + high, 2) == c)
+        def _():
+            swap_source.start()
+
+        if i == 0:
+            swap_p.start()
+            swap_q.start()
+
         if i == 1:
             @pl.when(k == 1)
             def _():
@@ -385,6 +388,7 @@
 
         if i == 0:
             compose()
+            send_screened()
 
     @pl.loop(2, 4)
     def _(i):
@@ -418,9 +422,9 @@
                 res[(b, e, 0) + at] = values[e][1]
                 res[(b, e, 1) + at] = values[e][0]
 
-        @pl.loop(1, ne)
-        def _(offset):
-            to = peer(offset)
+        @pl.loop(0, ne - 1)
+        def _(turn):
+            to = peer(turn)
             pltpu.make_async_remote_copy(
                 src_ref=res.at[b, to],
                 dst_ref=self_hbm.at[b, :, rows_of(me), :],

time: 101 us -> 99.2 us (0.982)
  Pallas kernels: 99.1 us -> 97.6 us
    pallas_call x1, Pallas kernels: 97 us -> 95.5 us  [per_device(): pl.pallas_call(functools.partial(kernel, ny, nx), out_shape=[jax.ShapeDty...]
where the time goes in v5:
time: 99.2 us; the launch traced here: 99.1 us
  Pallas kernels  97.6 us (98%)
    pallas_call x1, Pallas kernels, per_device(): pl.pallas_call(functools.partial(kernel, ny, nx), out_shape=[jax.ShapeDty...  95.5 us
    pallas_call x1, Pallas kernels, per_device(): pl.pallas_call(hand_over, out_shape=[jax.ShapeDtypeStruct(shape, F32)] *...  2.07 us

profile of v5, /device:TPU:1, one launch (start us, length us, event | category | flops | bytes accessed | tf_op | source)
XLA Modules:
  0.0 99.1 jit_solution(16618060547481464563)
XLA Ops:
  0.6 0.0 copy-start
  0.6 0.6 copy-done
  1.3 95.5 %shard_map.68 = (f32[4,2,256,256]{3,2,1,0:T(8,128)S(1)}, f32[4,2,256,256]{3,2,1,0:T(8,128)S(1)}) custom-call(f32[4,2,256,256]{3,2,1,0:T(8,128)} %bitcast.6, f32[4,2,256,256]{3,2,1,0:T(8,128)} %bitcast.7, f32[4,2,256,256]{3,2,1,0:T(8,128)} %bitcast.8, s32[1,4]{1,0:T(1,128)S(1)} %copy-done, f32[4,2,256,256]{3,2,1,0:T(8,128)} %bitcast.9), custom_call_target="tpu_custom_call" | custom-call | tf_op jit(solution)/shard_map/pallas_call | solution.py:482
  96.8 2.1 %shard_map.69 = (f32[4,2,256,256]{3,2,1,0:T(8,128)}, f32[4,2,256,256]{3,2,1,0:T(8,128)}) custom-call(f32[4,2,256,256]{3,2,1,0:T(8,128)S(1)} %get-tuple-element.6.diag_in, f32[4,2,256,256]{3,2,1,0:T(8,128)S(1)} %get-tuple-element.7.self_in), custom_call_target="tpu_custom_call" | custom-call | tf_op jit(solution)/shard_map/pallas_call | solution.py:518
Async XLA Ops:
  0.6 0.7 copy-start

commit v6 on v5

--- a/solution.py
+++ b/solution.py
@@ -196,12 +196,8 @@
             if direction == 1 and b > 0:
                 real, imag = product(CUR, X0 - j)
                 split_store(T1, real + af[j, 0], imag + af[j, 1])
-            if outer and b > 0:
-                real, imag = product(X0 - b, X0 + b - 1)
-                split_store(X0 + b, real, imag)
-                if b == BLOCKS - 1:
-                    pqf[0, 0] = real
-                    pqf[0, 1] = imag
+            if outer and 0 < b < BLOCKS - 1:
+                split_store(X0 + b, *product(X0 - b, X0 + b - 1))
             if direction == 0 and b > 0:
                 real, imag = product(T0, Y0 - b)
                 real, imag = real + gf[b, 0], imag + gf[b, 1]
@@ -214,12 +210,24 @@
             if b == BLOCKS - 1:
                 sf[direction, 0] = real
                 sf[direction, 1] = imag
+                if outer:
+                    pl.semaphore_wait(barrier, ne + neighbours)
+
+                @pl.when(c == direction)
+                def _():
+                    swap_source.start()
+
+            if outer and b == BLOCKS - 1:
+                real, imag = product(X0 - b, X0 + b - 1)
+                pqf[0, 0] = real
+                pqf[0, 1] = imag
+                split_store(X0 + b, real, imag)
             if outer and b > 0:
                 real, imag = product(Y0 + b - 1, Y0 - b)
-                split_store(Y0 + b, real, imag)
                 if b == BLOCKS - 1:
                     pqf[1, 0] = real
                     pqf[1, 1] = imag
+                split_store(Y0 + b, real, imag)
 
     def join():
         swap_source.wait_recv()
@@ -332,9 +340,9 @@
 
         @pl.when(jnp.logical_not(own) & (k < last))
         def _():
-            for half in forward:
-                half.wait_recv()
-            split_store(CUR, oi[0], oi[1])
+            for copy, half in zip(forward, halves):
+                copy.wait_recv()
+                split_store(CUR, oi[0, half], oi[1, half], half)
 
         @pl.when(jnp.logical_not(own) & (k == last))
         def _():
@@ -365,13 +373,6 @@
             @pl.when(high == side)
             def _():
                 chain((i + side) % 2, i == 0)
-
-        if i == 0:
-            pl.semaphore_wait(barrier, ne + neighbours)
-
-        @pl.when(lax.rem(i + high, 2) == c)
-        def _():
-            swap_source.start()
 
         if i == 0:
             swap_p.start()

time: 99.2 us -> 99.5 us (level)
  no operation moved by 1% of the time
where the time goes in v6:
time: 99.5 us; the launch traced here: 98.4 us
  Pallas kernels  96.9 us (97%)
    pallas_call x1, Pallas kernels, per_device(): pl.pallas_call(functools.partial(kernel, ny, nx), out_shape=[jax.ShapeDty...  94.9 us
    pallas_call x1, Pallas kernels, per_device(): pl.pallas_call(hand_over, out_shape=[jax.ShapeDtypeStruct(shape, F32)] *...  2.07 us

profile of v6, /device:TPU:1, one launch (start us, length us, event | category | flops | bytes accessed | tf_op | source)
XLA Modules:
  0.0 98.4 jit_solution(2920693537234110446)
XLA Ops:
  0.6 0.0 copy-start
  0.6 0.6 copy-done
  1.3 94.9 %shard_map.68 = (f32[4,2,256,256]{3,2,1,0:T(8,128)S(1)}, f32[4,2,256,256]{3,2,1,0:T(8,128)S(1)}) custom-call(f32[4,2,256,256]{3,2,1,0:T(8,128)} %bitcast.6, f32[4,2,256,256]{3,2,1,0:T(8,128)} %bitcast.7, f32[4,2,256,256]{3,2,1,0:T(8,128)} %bitcast.8, s32[1,4]{1,0:T(1,128)S(1)} %copy-done, f32[4,2,256,256]{3,2,1,0:T(8,128)} %bitcast.9), custom_call_target="tpu_custom_call" | custom-call | tf_op jit(solution)/shard_map/pallas_call | solution.py:483
  96.2 2.1 %shard_map.69 = (f32[4,2,256,256]{3,2,1,0:T(8,128)}, f32[4,2,256,256]{3,2,1,0:T(8,128)}) custom-call(f32[4,2,256,256]{3,2,1,0:T(8,128)S(1)} %get-tuple-element.6.diag_in, f32[4,2,256,256]{3,2,1,0:T(8,128)S(1)} %get-tuple-element.7.self_in), custom_call_target="tpu_custom_call" | custom-call | tf_op jit(solution)/shard_map/pallas_call | solution.py:519
Async XLA Ops:
  0.6 0.7 copy-start
